TPU v7x, 256 devices: a whole 4x4x8 slice. The times are simulated.
256 devices in a mesh: group: 8 (over z_lo, y), dev: 32 (over x, z_hi, core).
Axes of the slice: x: 4, y: 4, z: 8 (z_hi: 4, z_lo: 2; z = z_hi * 2 + z_lo), core: 2. Of those that a mesh axis runs over, the one named last changes fastest.
Arguments:
- stored_q: float32 [8, 192, 8192], P('group', 'dev'), may hold values from -1.75 to 1.75
- stored_kv: float32 [8, 64, 16384], P('group', 'dev'), may hold values from -1.75 to 1.75
- stored_o: float32 [8, 448, 8192], P('group', 'dev'), may hold values from -1.75 to 1.75
- owner_map: int32 [32, 8], replicated, may hold values from 0 to 7, each once within a row
Outputs:
- q_fold: bfloat16 [64, 1536, 512], P('dev')
- o_fold: bfloat16 [64, 512, 3584], P('dev')
Inputs may be any that keep to these rules, and one draw needn't show every extreme that they name: Each row of owner_map names every trainer slot once.
All inputs are finite; a program needn't handle non-finite values.
Results may differ from a plain program's by a relative error of at most 0.001.
Values may be sent and summed in bfloat16 or wider, within the bound.
A program may use at most 128 MiB of HBM per device.

v0:
```python
import jax
import jax.numpy as jnp
from jax import lax
from jax.sharding import PartitionSpec as P

HD = 128


def take_slots(values, owner_row):
    slot_count = owner_row.shape[0]
    grouped = values.reshape(slot_count, values.shape[0] // slot_count, values.shape[1])
    return jnp.take(grouped, owner_row, axis=0).reshape(values.shape)


def fold_heads(query_rows, latent, output):
    heads = query_rows.shape[1] // HD
    query3 = query_rows.reshape(query_rows.shape[0], heads, HD)
    latent4 = latent.reshape(latent.shape[0], heads, 2, HD)
    out3 = output.reshape(output.shape[0], heads, HD)
    q_part = jnp.einsum("rhe,che->hrc", query3, latent4[:, :, 0], precision=lax.Precision.HIGHEST)
    o_part = jnp.einsum("che,whe->hcw", latent4[:, :, 1], out3, precision=lax.Precision.HIGHEST)
    return (q_part.astype(jnp.bfloat16), o_part.astype(jnp.bfloat16))


def body(stored_q, stored_kv, stored_o, owner_map):
    pieces = (stored_q[0], stored_kv[0], stored_o[0])
    owner_row = lax.dynamic_index_in_dim(owner_map, lax.axis_index("dev"), 0, keepdims=False)
    gathered = (
        lax.all_gather(pieces[0], "group", axis=0, tiled=True),
        lax.all_gather(pieces[1], "group", axis=0, tiled=True),
        lax.all_gather(pieces[2], "group", axis=0, tiled=True),
    )
    segments = tuple((take_slots(member, owner_row) for member in gathered))
    query_rows, latent, output = (
        lax.all_to_all(segments[0], "dev", split_axis=1, concat_axis=0, tiled=True),
        lax.all_to_all(segments[1], "dev", split_axis=1, concat_axis=0, tiled=True),
        lax.all_to_all(segments[2], "dev", split_axis=1, concat_axis=0, tiled=True),
    )
    q_fold, o_fold = fold_heads(query_rows, latent, output)
    return (q_fold, o_fold)


def solution(mesh):
    in_specs = (P("group", "dev", None), P("group", "dev", None), P("group", "dev", None), P())
    out_specs = (P("dev", None, None), P("dev", None, None))
    return jax.shard_map(body, mesh=mesh, in_specs=in_specs, out_specs=out_specs, check_vma=False)
```

profile of v0, /device:TPU:33, one launch (start us, length us, event | category | flops | bytes accessed | tf_op | source)
XLA Modules:
  0.0 351.6 jit_solution(1678190973396665944)
XLA Ops:
  7.2 1.7 copy.20
  9.0 0.7 all-gather.7.cloned.1.call-update
  9.7 0.7 all-gather.11.cloned.1.call-update
  10.8 37.4 %all-gather.9.cloned.1.call-done = f32[1,16,16384]{2,0,1:T(1,128)} async-done(((f32[1,2,16384]{2,0,1:T(1,128)}), f32[1,16,16384]{2,0,1:T(1,128)}) %all-gather.9.cloned.1.call-update) | async-done | bytes 1048592 | tf_op jit(solution)/shard_map/all_gather | solution.py:30
  48.3 3.9 %reduce.3 = f32[16,16384]{1,0:T(8,128)S(1)} reduce(f32[1,16,16384]{2,0,1:T(1,128)} %all-gather.9.cloned.1.call-done, f32[]{:T(128)} %constant.53), dimensions={0}, to_apply=%all-gather.1.reduce_sub_computation | reduce | bytes 2097156 | tf_op jit(solution)/shard_map/all_gather | solution.py:30
  52.1 0.6 reshape.97
  52.8 1.7 gather_fusion.1
  54.4 0.9 gather.21
  55.5 1.6 copy.21
  57.1 15.5 %all-to-all-start.1 = ((f32[16,32,512]{2,0,1:T(8,128)}), f32[16,32,512]{2,0,1:T(8,128)S(1)}, u32[]{:S(2)}, u32[]{:S(2)}) async-start(f32[16,32,512]{2,0,1:T(8,128)} %copy.21), calls=%async_computation.1 | async-start | bytes 2097152 | tf_op jit(solution)/shard_map/all_to_all | solution.py:36
  72.7 34.9 %all-gather.7.cloned.1.call-done = f32[1,48,8192]{2,0,1:T(1,128)} async-done(((f32[1,6,8192]{2,0,1:T(1,128)}), f32[1,48,8192]{2,0,1:T(1,128)}) %all-gather.7.cloned.1.call-update) | async-done | bytes 1572880 | tf_op jit(solution)/shard_map/all_gather | solution.py:29
  107.6 6.5 %reduce.1 = f32[48,8192]{1,0:T(8,128)} reduce(f32[1,48,8192]{2,0,1:T(1,128)} %all-gather.7.cloned.1.call-done, f32[]{:T(128)} %constant.53), dimensions={0}, to_apply=%all-gather.reduce_sub_computation | reduce | bytes 3145732 | tf_op jit(solution)/shard_map/all_gather | solution.py:29
  114.1 1.6 reshape.95
  115.7 2.0 gather_fusion
  117.7 2.2 gather.19
  120.1 2.1 copy.19
  122.1 12.1 %all-to-all-start = ((f32[48,32,256]{2,0,1:T(8,128)}), f32[48,32,256]{2,0,1:T(8,128)S(1)}, u32[]{:S(2)}, u32[]{:S(2)}) async-start(f32[48,32,256]{2,0,1:T(8,128)} %copy.19), calls=%async_computation | async-start | bytes 3145728 | tf_op jit(solution)/shard_map/all_to_all | solution.py:35
  134.4 60.9 %all-gather.11.cloned.1.call-done = f32[1,112,8192]{2,0,1:T(1,128)} async-done(((f32[1,14,8192]{2,0,1:T(1,128)}), f32[1,112,8192]{2,0,1:T(1,128)}) %all-gather.11.cloned.1.call-update) | async-done | bytes 3670032 | tf_op jit(solution)/shard_map/all_gather | solution.py:31
  195.3 12.2 %reduce.4 = f32[112,8192]{1,0:T(8,128)} reduce(f32[1,112,8192]{2,0,1:T(1,128)} %all-gather.11.cloned.1.call-done, f32[]{:T(128)} %constant.53), dimensions={0}, to_apply=%all-gather.2.reduce_sub_computation | reduce | bytes 7340036 | tf_op jit(solution)/shard_map/all_gather | solution.py:31
  207.5 3.7 %reshape.99 = f32[8,14,8192]{2,1,0:T(8,128)} reshape(f32[112,8192]{1,0:T(8,128)} %reduce.4) | data formatting | bytes 7340032 | tf_op jit(solution)/shard_map/reshape | solution.py:11
  211.3 4.9 %gather_fusion.2 = f32[8,14,8192]{2,1,0:T(8,128)} fusion(f32[8,14,8192]{2,1,0:T(8,128)} %reshape.99, s32[1024]{0:T(1024)S(1)} %pad_clamp_fusion), kind=kCustom, calls=%fused_computation.2 | custom fusion | bytes 7340064 | tf_op jit(solution)/shard_map/jit(_take)/gather | solution.py:12
  216.2 5.0 %gather.23 = f32[112,32,256]{2,1,0:T(8,128)} reshape(f32[8,14,8192]{2,1,0:T(8,128)} %gather_fusion.2) | data formatting | bytes 7340032 | tf_op jit(solution)/shard_map/jit(_take)/gather | solution.py:12
  221.3 2.4 broadcast_select_fusion
  223.6 4.0 %copy.25 = f32[112,32,256]{2,0,1:T(8,128)} copy(f32[112,32,256]{2,1,0:T(8,128)S(1)} %broadcast_select_fusion) | data formatting | bytes 7340032 | tf_op jit(solution)/shard_map/jit(_take)/select_n | solution.py:12
  227.6 10.3 %all-to-all-start.2 = ((f32[112,32,256]{2,0,1:T(8,128)}), f32[112,32,256]{2,0,1:T(8,128)}, u32[]{:S(2)}, u32[]{:S(2)}) async-start(f32[112,32,256]{2,0,1:T(8,128)} %copy.25), calls=%async_computation.2 | async-start | bytes 7340032 | tf_op jit(solution)/shard_map/all_to_all | solution.py:37
  237.9 1.6 reshape.98
  239.5 3.4 fusion.3
  242.9 0.8 reshape.96
  243.8 7.5 %convolution_convert_fusion.1 = bf16[2,1536,512]{2,1,0:T(8,128)(2,1)} fusion(f32[1536,2,128]{2,1,0:T(2,128)S(1)} %reshape.96, f32[512,2,1,128]{3,2,1,0:T(1,128)} %get-tuple-element.3), kind=kOutput, calls=%fused_computation.4 | convolution fusion | flops 2417491968 | bytes 5242880 | tf_op jit(solution)/shard_map/rhe,che->hrc/dot_general | solution.py:20
  251.3 72.8 %all-to-all-done.2 = f32[112,32,256]{2,0,1:T(8,128)} async-done(((f32[112,32,256]{2,0,1:T(8,128)}), f32[112,32,256]{2,0,1:T(8,128)}, u32[]{:S(2)}, u32[]{:S(2)}) %all-to-all-start.2) | async-done | bytes 3670048 | tf_op jit(solution)/shard_map/all_to_all | solution.py:37
  324.1 5.5 %reshape.100 = f32[3584,2,128]{2,1,0:T(2,128)} reshape(f32[32,112,256]{2,1,0:T(8,128)} %bitcast.5) | data formatting | bytes 7340032 | tf_op jit(solution)/shard_map/reshape | solution.py:19
  329.6 15.5 %convolution_convert_fusion = bf16[2,512,3584]{2,1,0:T(8,128)(2,1)} fusion(f32[3584,2,128]{2,1,0:T(2,128)} %reshape.100, f32[512,2,1,128]{3,2,1,0:T(1,128)S(1)} %copy-done.2), kind=kOutput, calls=%fused_computation.3 | convolution fusion | flops 5640814592 | bytes 11534336 | tf_op jit(solution)/shard_map/che,whe->hcw/dot_general | solution.py:21
  (24 shorter events, 1.2 us)
Async XLA Ops:
  7.2 3.3 copy-start
  7.2 41.1 %all-gather.9.cloned.1.call-start = ((), (), s32[]{:S(2)}) async-start(), calls=%async_computation.4 | async-start | bytes 1179648 | tf_op jit(solution)/shard_map/all_gather | solution.py:30
  8.9 98.7 %all-gather.7.cloned.1.call-start = ((), (), s32[]{:S(2)}) async-start(), calls=%async_computation.3 | async-start | bytes 1769472 | tf_op jit(solution)/shard_map/all_gather | solution.py:29
  9.7 185.6 %all-gather.11.cloned.1.call-start = ((), (), s32[]{:S(2)}) async-start(), calls=%async_computation.5 | async-start | bytes 4128768 | tf_op jit(solution)/shard_map/all_gather | solution.py:31
  57.1 65.0 %all-to-all-start.1 = ((f32[16,32,512]{2,0,1:T(8,128)}), f32[16,32,512]{2,0,1:T(8,128)S(1)}, u32[]{:S(2)}, u32[]{:S(2)}) async-start(f32[16,32,512]{2,0,1:T(8,128)} %copy.21), calls=%async_computation.1 | async-start | bytes 2097152 | tf_op jit(solution)/shard_map/all_to_all | solution.py:36
  122.1 105.5 %all-to-all-start = ((f32[48,32,256]{2,0,1:T(8,128)}), f32[48,32,256]{2,0,1:T(8,128)S(1)}, u32[]{:S(2)}, u32[]{:S(2)}) async-start(f32[48,32,256]{2,0,1:T(8,128)} %copy.19), calls=%async_computation | async-start | bytes 3145728 | tf_op jit(solution)/shard_map/all_to_all | solution.py:35
  227.6 96.6 %all-to-all-start.2 = ((f32[112,32,256]{2,0,1:T(8,128)}), f32[112,32,256]{2,0,1:T(8,128)}, u32[]{:S(2)}, u32[]{:S(2)}) async-start(f32[112,32,256]{2,0,1:T(8,128)} %copy.25), calls=%async_computation.2 | async-start | bytes 7340032 | tf_op jit(solution)/shard_map/all_to_all | solution.py:37
  324.1 5.5 %copy-start.2 = (f32[512,2,1,128]{3,2,1,0:T(1,128)S(1)}, f32[512,2,1,128]{3,2,1,0:T(1,128)}, u32[]{:S(2)}) copy-start(f32[512,2,1,128]{3,2,1,0:T(1,128)} %get-tuple-element.2) | copy-start | bytes 1572868
  329.6 15.5 %copy-start.1 = (s32[32,8]{0,1:T(8,128)S(1)}, s32[32,8]{0,1:T(8,128)}, u32[]{:S(2)}) copy-start(s32[32,8]{0,1:T(8,128)} %param.7) | copy-start | bytes 3076
Sparse Core Ops, SparseCore 0:
  10.4 37.8 all-gather.8
  50.1 57.5 all-gather.6
  109.4 85.8 all-gather.10
where the time goes:
time: 352 us
  waiting for transfers between devices  208 us (59%)
  local copies, waits for them, and re-layouts  44 us (12%)
  starting transfers between devices  38 us (11%)
  other arithmetic  25.2 us (7%)
  matrix products  23 us (7%)
  between operations  13.9 us (4%)
    all_to_all x1, waiting for transfers between devices, body(): lax.all_to_all(segments[2], 'dev', split_axis=1, concat_axis=0, tiled=True)  72.8 us
    all_gather x1, waiting for transfers between devices, body(): lax.all_gather(pieces[2], 'group', axis=0, tiled=True)  60.9 us
    all_gather x1, waiting for transfers between devices, body(): lax.all_gather(pieces[1], 'group', axis=0, tiled=True)  37.4 us
    all_gather x1, waiting for transfers between devices, body(): lax.all_gather(pieces[0], 'group', axis=0, tiled=True)  34.9 us
    gather x6, local copies, waits for them, and re-layouts, take_slots(): return jnp.take(grouped, owner_row, axis=0).reshape(values.shape)  16.7 us
    all_to_all x1, starting transfers between devices, body(): lax.all_to_all(segments[1], 'dev', split_axis=1, concat_axis=0, tiled=True)  15.5 us
    dot_general x1, matrix products, fold_heads(): jnp.einsum('che,whe->hcw', latent4[:, :, 1], out3, precision=lax.Precisio...  15.5 us
    all_gather x1, other arithmetic, body(): lax.all_gather(pieces[2], 'group', axis=0, tiled=True)  12.2 us
  transfers between devices with their start and end apart: 6, of which 4 were waited for; matrix products, arithmetic and copies ran while one was open for 20% of the time, Pallas kernels for 0%

commit v1 on v0

v1 whole, which is shorter than its diff:
```python
import jax
import jax.numpy as jnp
from jax import lax
from jax.experimental import pallas as pl
from jax.experimental.pallas import tpu as pltpu
from jax.sharding import PartitionSpec as P

MESH = pl.DeviceIdType.MESH
F32, BF16, I32 = jnp.float32, jnp.bfloat16, jnp.int32
NG, ND = 8, 32
ROWS = 16
GROW = 1.008 / 32767.0
LEAST = 2.0**-120


def nt(a, b):
    return lax.dot_general(a, b, (((1,), (1,)), ((), ())), preferred_element_type=F32)


def kernel(q_ref, kv_ref, o_ref, own_ref, qf_ref, of_ref,
           send, ssend, gat, gsc, sca, jmap, inv, qm, km, om, vm,
           a_send, a_recv, s_send, s_recv):
    g = lax.axis_index("group")
    d = lax.axis_index("dev")
    zl, y = g // 4, g % 4
    up, down, far = (y + 1) % 4, (y + 3) % 4, (y + 2) % 4
    mine, other = zl * 4, (1 - zl) * 4
    near = {"z": (other + y, d), "p": (mine + up, d), "m": (mine + down, d)}

    barrier = pltpu.get_barrier_semaphore()

    def greet(i, _):
        pl.semaphore_signal(barrier, inc=1, device_id=(g, (d + i) % ND), device_id_type=MESH)
        return 0

    lax.fori_loop(1, ND, greet, 0)
    for who in near.values():
        pl.semaphore_signal(barrier, inc=1, device_id=who, device_id_type=MESH)

    row = lax.broadcasted_iota(I32, (ROWS, 128), 0)
    lane = lax.broadcasted_iota(I32, (ROWS, 128), 1)

    def quantise(i, _):
        c0 = pl.multiple_of(i * 256, 256)
        c1 = pl.multiple_of(i * 512, 512)
        qs = [q_ref[0, :, pl.ds(c0 + 128 * h, 128)] for h in range(2)]
        os = [o_ref[0, :, pl.ds(c0 + 128 * h, 128)] for h in range(2)]
        ks = [kv_ref[0, :, pl.ds(c1 + 128 * h, 128)] for h in range(4)]
        blocks = (
            jnp.concatenate([qs[0], qs[1], ks[0], ks[2]], axis=0),
            jnp.concatenate([os[0], ks[1]], axis=0),
            jnp.concatenate([os[1], ks[3]], axis=0),
        )
        packed = jnp.zeros((1, 128), F32)
        for t, x in enumerate(blocks):
            top = jnp.max(jnp.abs(x), axis=1, keepdims=True)
            scale = jnp.maximum((top * GROW).astype(BF16).astype(F32), LEAST)
            code = jnp.round(x * (1.0 / scale)).astype(I32)
            send[t, i] = code.astype(jnp.int16)
            spread = jnp.where(lane == row + ROWS * t, scale, 0.0)
            packed = packed + jnp.sum(spread, axis=0, keepdims=True)
        ssend[i] = packed
        return 0

    lax.fori_loop(0, ND, quantise, 0, unroll=2)
    pl.semaphore_wait(barrier, ND + 2)

    def out_of(t):
        return ssend if t == 3 else send.at[t]

    def into(t, group):
        return gsc.at[group] if t == 3 else gat.at[t, group]

    def exchange(t):
        src, dst = out_of(t), into(t, g)

        def one(i, _):
            to = (d + i) % ND
            pltpu.make_async_remote_copy(
                src_ref=src.at[to], dst_ref=dst.at[d], send_sem=a_send.at[t], recv_sem=a_recv.at[t],
                device_id=(g, to), device_id_type=MESH).start()
            return 0

        lax.fori_loop(1, ND, one, 0)
        if t == 3:
            gsc[g, d] = ssend[d]
        else:
            gat[t, g, d] = send[t, d]

    for t in (0, 3, 1, 2):
        exchange(t)

    r = lax.broadcasted_iota(I32, (128, 128), 0)
    k = lax.broadcasted_iota(I32, (128, 128), 1)
    kin = k - (k // ROWS) * ROWS

    def piece(rem, size):
        return sum(((rem >= size * n).astype(I32) for n in range(1, NG)), jnp.zeros_like(rem))

    h1 = (r >= 48).astype(I32)
    rq = r - 48 * h1
    jq = piece(rq, 6)
    h2 = (r >= 112).astype(I32)
    rk = r - 96 - 16 * h2
    jk = piece(rk, 2)
    offset = jnp.where(r < 96, rq - 6 * jq + 6 * h1, rk - 2 * jk + 12 + 2 * h2)
    jmap[0] = jnp.where(offset == kin, jnp.where(r < 96, jq, jk), -1)
    jo = piece(r, 14)
    rv = r - 112
    jv = piece(rv, 2)
    offset = jnp.where(r < 112, r - 14 * jo, rv - 2 * jv + 14)
    jmap[1] = jnp.where(offset == kin, jnp.where(r < 112, jo, jv), -1)
    kg = lax.broadcasted_iota(I32, (ND, 128), 1) // ROWS
    held = jnp.zeros((ND, 128), I32)
    for j in range(NG):
        held = held + jnp.where(own_ref[:, j:j + 1] == kg, j, 0)
    inv[...] = held

    def hop(t, kind, ref, who):
        n = t * 9 + kind
        return pltpu.make_async_remote_copy(
            src_ref=ref, dst_ref=ref, send_sem=s_send.at[n], recv_sem=s_recv.at[n],
            device_id=who, device_id_type=MESH)

    started = []

    def go(*args):
        c = hop(*args)
        c.start()
        started.append(c)

    def half(t, group, n):
        return into(t, group).at[pl.ds(n * (ND // 2), ND // 2)]

    def own(t):
        whole = into(t, g).at[pl.ds(0, ND - 1)]
        pltpu.make_async_copy(whole, whole, a_recv.at[t]).wait()
        go(t, 0, into(t, g), near["z"])
        go(t, 1, into(t, g), near["p"])
        go(t, 2, into(t, g), near["m"])

    def partner(t):
        ref = into(t, other + y)
        hop(t, 0, ref, near["z"]).wait_recv()
        go(t, 3, ref, near["p"])
        go(t, 4, ref, near["m"])

    def forward(t, b):
        base = (mine, other)[b]
        hop(t, 1 + 2 * b, into(t, base + down), near["p"]).wait_recv()
        go(t, 5 + 2 * b, half(t, base + down, 0), near["p"])
        hop(t, 2 + 2 * b, into(t, base + up), near["m"]).wait_recv()
        go(t, 6 + 2 * b, half(t, base + up, 1), near["m"])

    def finish(t):
        for b, base in enumerate((mine, other)):
            hop(t, 5 + 2 * b, half(t, base + far, 0), near["p"]).wait_recv()
            hop(t, 6 + 2 * b, half(t, base + far, 1), near["m"]).wait_recv()

    def scales():
        at = lax.broadcasted_iota(I32, (1, 128), 1) // ROWS

        def one(i, _):
            for t in range(3):
                line = jnp.zeros((1, 128), F32)
                for n in range(NG):
                    line = line + jnp.where(at == n, pltpu.roll(gsc[n, i], (ROWS * (n - t)) % 128, 1), 0.0)
                sca[t, i] = line
            return 0

        lax.fori_loop(0, ND, one, 0)

    def decode(t, i):
        code = gat[t, :, i].reshape(128, 128).astype(F32)
        hi = code.astype(BF16)
        lo = (code - hi.astype(F32)).astype(BF16)
        pick = jnp.where(jmap[min(t, 1)] == inv[pl.ds(i, 1), :], sca[t, i], 0.0).astype(BF16)
        got = jnp.dot(pick, jnp.concatenate([hi, lo], axis=1), preferred_element_type=F32)
        x = got[:, :128] + got[:, 128:]
        hi = x.astype(BF16)
        return hi, (x - hi.astype(F32)).astype(BF16)

    def queries():
        def one(i, _):
            hi, lo = decode(0, i)
            at = pl.ds(pl.multiple_of(i * 48, 16), 48)
            kat = pl.ds(pl.multiple_of(i * 16, 16), 16)
            for h in range(2):
                qm[h, at, 0:128] = hi[48 * h:48 * h + 48]
                qm[h, at, 128:256] = lo[48 * h:48 * h + 48]
                s = slice(96 + 16 * h, 112 + 16 * h)
                km[h, kat, 0:128] = hi[s]
                km[h, kat, 128:256] = hi[s]
                km[h, kat, 256:384] = lo[s]
            return 0

        lax.fori_loop(0, ND, one, 0)
        for h in range(2):
            def tile(i, _):
                at = pl.ds(pl.multiple_of(i * 256, 256), 256)
                x = nt(qm[h, at, :], km[h, :, 0:256]) + nt(qm[h, at, 0:128], km[h, :, 256:384])
                qf_ref[h, at, :] = x.astype(BF16)
                return 0

            lax.fori_loop(0, 6, tile, 0)

    def outputs(h):
        def one(i, _):
            hi, lo = decode(1 + h, i)
            at = pl.ds(pl.multiple_of(i * 112, 16), 112)
            vat = pl.ds(pl.multiple_of(i * 16, 16), 16)
            om[at, 0:128] = hi[:112]
            om[at, 128:256] = hi[:112]
            om[at, 256:384] = lo[:112]
            vm[vat, 0:128] = hi[112:]
            vm[vat, 128:256] = lo[112:]
            return 0

        lax.fori_loop(0, ND, one, 0)

        def tile(i, _):
            at = pl.ds(pl.multiple_of(i * 256, 256), 256)
            x = nt(vm[...], om[at, 0:256]) + nt(vm[:, 0:128], om[at, 256:384])
            of_ref[h, :, at] = x.astype(BF16)
            return 0

        lax.fori_loop(0, 14, tile, 0)

    own(0)
    own(3)
    own(1)
    partner(0)
    partner(3)
    own(2)
    forward(0, 0)
    forward(3, 0)
    partner(1)
    forward(0, 1)
    forward(3, 1)
    partner(2)
    forward(1, 0)
    finish(0)
    finish(3)
    scales()
    queries()
    forward(1, 1)
    forward(2, 0)
    finish(1)
    outputs(0)
    forward(2, 1)
    finish(2)
    outputs(1)
    for c in started:
        c.wait_send()
    for t in range(4):
        sent = out_of(t).at[pl.ds(0, ND - 1)]
        pltpu.make_async_copy(sent, sent, a_send.at[t]).wait()


def body(stored_q, stored_kv, stored_o, owner_map):
    vmem = pl.BlockSpec(memory_space=pltpu.VMEM)
    return pl.pallas_call(
        kernel,
        out_shape=(pltpu.VMEM((2, 1536, 512), BF16), pltpu.VMEM((2, 512, 3584), BF16)),
        in_specs=[vmem] * 4,
        out_specs=(vmem, vmem),
        scratch_shapes=[
            pltpu.VMEM((3, ND, ROWS, 128), jnp.int16),
            pltpu.VMEM((ND, 1, 128), F32),
            pltpu.VMEM((3, NG, ND, ROWS, 128), jnp.int16),
            pltpu.VMEM((NG, ND, 1, 128), F32),
            pltpu.VMEM((3, ND, 1, 128), F32),
            pltpu.VMEM((2, 128, 128), I32),
            pltpu.VMEM((ND, 128), I32),
            pltpu.VMEM((2, 1536, 256), BF16),
            pltpu.VMEM((2, 512, 384), BF16),
            pltpu.VMEM((3584, 384), BF16),
            pltpu.VMEM((512, 256), BF16),
            pltpu.SemaphoreType.DMA((4,)),
            pltpu.SemaphoreType.DMA((4,)),
            pltpu.SemaphoreType.DMA((36,)),
            pltpu.SemaphoreType.DMA((36,)),
        ],
        compiler_params=pltpu.CompilerParams(
            collective_id=0, has_side_effects=True, vmem_limit_bytes=40 * 1024 * 1024),
    )(stored_q, stored_kv, stored_o, owner_map)


def solution(mesh):
    in_specs = (P("group", "dev", None), P("group", "dev", None), P("group", "dev", None), P())
    out_specs = (P("dev", None, None), P("dev", None, None))
    return jax.shard_map(body, mesh=mesh, in_specs=in_specs, out_specs=out_specs, check_vma=False)
```

time: 352 us -> 87.9 us (0.25)
  the two profiles are of different devices: /device:TPU:33 before, /device:TPU:6 now
where the time goes in v1:
time: 87.9 us; the launch traced here: 86.9 us
  Pallas kernels  77.6 us (88%)
  local copies, waits for them, and re-layouts  8.72 us (10%)
    pallas_call x1, Pallas kernels, body(): pl.pallas_call(kernel, out_shape=(pltpu.VMEM((2, 1536, 512), BF16), pltpu...  77.6 us
    unnamed x7, local copies, waits for them, and re-layouts  8.72 us

profile of v1, /device:TPU:6, one launch (start us, length us, event | category | flops | bytes accessed | tf_op | source)
XLA Modules:
  0.0 86.9 jit_solution(2752117500790444988)
XLA Ops:
  0.6 0.8 copy.8.own_ref
  1.4 1.0 %copy.6.q_ref = f32[1,6,8192]{2,1,0:T(8,128)S(1)} copy(f32[1,6,8192]{2,0,1:T(1,128)} %param.4) | data formatting | bytes 393216 | tf_op args[0]
  2.4 1.3 %copy.7.o_ref = f32[1,14,8192]{2,1,0:T(8,128)S(1)} copy(f32[1,14,8192]{2,0,1:T(1,128)} %param.6) | data formatting | bytes 917504 | tf_op args[2]
  3.7 0.0 copy-start
  3.7 0.9 %copy-done = f32[1,2,16384]{2,1,0:T(2,128)S(1)} copy-done((f32[1,2,16384]{2,1,0:T(2,128)S(1)}, f32[1,2,16384]{2,1,0:T(2,128)}, u32[]{:S(2)}) %copy-start) | copy-done | bytes 131096
  4.6 77.6 %shard_map.59 = (bf16[2,1536,512]{2,1,0:T(8,128)(2,1)S(1)}, bf16[2,512,3584]{2,1,0:T(8,128)(2,1)S(1)}) custom-call(f32[1,6,8192]{2,1,0:T(8,128)S(1)} %copy.6.q_ref, f32[1,2,16384]{2,1,0:T(2,128)S(1)} %copy-done, f32[1,14,8192]{2,1,0:T(8,128)S(1)} %copy.7.o_ref, s32[32,8]{1,0:T(8,128)S(1)} %copy.8.own_ref), custom_call_target="tpu_custom_call" | custom-call | tf_op jit(solution)/shard_map/pallas_call | solution.py:262
  82.2 1.7 %copy.11 = bf16[2,1536,512]{2,1,0:T(8,128)(2,1)} copy(bf16[2,1536,512]{2,1,0:T(8,128)(2,1)S(1)} %get-tuple-element.2) | data formatting | bytes 6291456
  83.9 3.0 %copy.12 = bf16[2,512,3584]{2,1,0:T(8,128)(2,1)} copy(bf16[2,512,3584]{2,1,0:T(8,128)(2,1)S(1)} %get-tuple-element.3) | data formatting | bytes 14680064
Async XLA Ops:
  3.7 0.9 %copy-start = (f32[1,2,16384]{2,1,0:T(2,128)S(1)}, f32[1,2,16384]{2,1,0:T(2,128)}, u32[]{:S(2)}) copy-start(f32[1,2,16384]{2,1,0:T(2,128)} %kv_ref.1) | copy-start | bytes 393220

commit v2 on v0

v2 whole, which is shorter than its diff:
```python
import jax
import jax.numpy as jnp
from jax import lax
from jax.experimental import pallas as pl
from jax.experimental.pallas import tpu as pltpu
from jax.sharding import PartitionSpec as P

MESH = pl.DeviceIdType.MESH
F32, BF16, I32 = jnp.float32, jnp.bfloat16, jnp.int32
NG, ND = 8, 32
ROWS = 16
NEAR, FAR = 8, 24
GROW = 1.008 / 32767.0
LEAST = 2.0**-120


def nt(a, b):
    return lax.dot_general(a, b, (((1,), (1,)), ((), ())), preferred_element_type=F32)


def fold_out(v, o):
    return (nt(v[:, 0:256], o[:, 0:256]) + nt(v[:, 0:128], o[:, 256:384])).astype(BF16)


def kernel(q_hbm, kv_hbm, o_hbm, own_ref, qf_ref, of_ref, om1, vm1,
           q_ref, kv_ref, o_ref, near, nsc, send, ssend, gat, gsc, sca, jmap, inv, qm, km, om0, vm0,
           in_sem, a_send, a_recv, x_send, x_recv, s_send, s_recv):
    loads = [pltpu.make_async_copy(a, b, in_sem.at[n])
             for n, (a, b) in enumerate(((q_hbm, q_ref), (kv_hbm, kv_ref), (o_hbm, o_ref)))]
    for c in loads:
        c.start()
    g = lax.axis_index("group")
    d = lax.axis_index("dev")
    zl, y = g // 4, g % 4
    zh, xc = (d // 2) % 4, (d // 8) * 2 + d % 2
    up, down, far = (y + 1) % 4, (y + 3) % 4, (y + 2) % 4
    mine, other = zl * 4, (1 - zl) * 4
    to_z, to_p, to_m = (other + y, d), (mine + up, d), (mine + down, d)

    def dev_at(z, n):
        return ((n // 2) * 4 + z) * 2 + n % 2

    barrier = pltpu.get_barrier_semaphore()

    def greet(i, _):
        pl.semaphore_signal(barrier, inc=1, device_id=(g, (d + i) % ND), device_id_type=MESH)
        return 0

    lax.fori_loop(1, ND, greet, 0)
    for who in (to_z, to_p, to_m):
        pl.semaphore_signal(barrier, inc=1, device_id=who, device_id_type=MESH)

    row = lax.broadcasted_iota(I32, (ROWS, 128), 0)
    lane = lax.broadcasted_iota(I32, (ROWS, 128), 1)

    def quantise(i):
        qs = [q_ref[:, 2 * i + h, :] for h in range(2)]
        os = [o_ref[:, 2 * i + h, :] for h in range(2)]
        ks = [kv_ref[i, 2 * h:2 * h + 2, :] for h in range(4)]
        blocks = (
            jnp.concatenate([qs[0], qs[1], ks[0], ks[2]], axis=0),
            jnp.concatenate([os[0], ks[1]], axis=0),
            jnp.concatenate([os[1], ks[3]], axis=0),
        )
        codes, packed = [], jnp.zeros((1, 128), F32)
        for t, x in enumerate(blocks):
            top = jnp.max(jnp.abs(x), axis=1, keepdims=True)
            scale = jnp.maximum((top * GROW).astype(BF16).astype(F32), LEAST)
            codes.append(jnp.round(x * (1.0 / scale)).astype(I32).astype(jnp.int16))
            spread = jnp.where(lane == row + ROWS * ((t + g) % NG), scale, 0.0)
            packed = packed + jnp.sum(spread, axis=0, keepdims=True)
        return codes, packed

    def code_near(n, _):
        codes, packed = quantise(dev_at(zh, n))
        for t in range(3):
            near[t, g, n] = codes[t]
        nsc[g, n] = packed
        return 0

    def code_far(n, _):
        codes, packed = quantise(dev_at((zh + 1 + n // NEAR) % 4, n % NEAR))
        for t in range(3):
            send[t, n] = codes[t]
        ssend[n] = packed
        return 0

    for c in loads:
        c.wait()
    lax.fori_loop(0, NEAR, code_near, 0, unroll=2)
    lax.fori_loop(0, FAR, code_far, 0, unroll=2)
    pl.semaphore_wait(barrier, ND + 2)

    def into(part, group):
        if part < 4:
            return nsc.at[group] if part == 3 else near.at[part, group]
        ref = gsc.at[group] if part == 7 else gat.at[part - 4, group]
        return ref.at[pl.ds(NEAR, FAR)]

    def half(part, group, n):
        size = (NEAR if part < 4 else FAR) // 2
        return into(part, group).at[pl.ds(n * size, size)]

    def hop(part, kind, ref, who):
        n = part * 9 + kind
        return pltpu.make_async_remote_copy(
            src_ref=ref, dst_ref=ref, send_sem=s_send.at[n], recv_sem=s_recv.at[n],
            device_id=who, device_id_type=MESH)

    started = []

    def go(*args):
        c = hop(*args)
        c.start()
        started.append(c)

    def own(part):
        go(part, 0, into(part, g), to_z)
        go(part, 1, into(part, g), to_p)
        go(part, 2, into(part, g), to_m)

    def partner(part):
        ref = into(part, other + y)
        hop(part, 0, ref, to_z).wait_recv()
        go(part, 3, ref, to_p)
        go(part, 4, ref, to_m)

    def forward(part, b):
        base = (mine, other)[b]
        hop(part, 1 + 2 * b, into(part, base + down), to_p).wait_recv()
        go(part, 5 + 2 * b, half(part, base + down, 0), to_p)
        hop(part, 2 + 2 * b, into(part, base + up), to_m).wait_recv()
        go(part, 6 + 2 * b, half(part, base + up, 1), to_m)

    def finish(part):
        for b, base in enumerate((mine, other)):
            hop(part, 5 + 2 * b, half(part, base + far, 0), to_p).wait_recv()
            hop(part, 6 + 2 * b, half(part, base + far, 1), to_m).wait_recv()

    def far_out(t):
        src = ssend if t == 3 else send.at[t]
        dst = gsc.at[g] if t == 3 else gat.at[t, g]

        def one(k, _):
            rel, n = k // NEAR, (xc + k) % NEAR
            pltpu.make_async_remote_copy(
                src_ref=src.at[rel * NEAR + n], dst_ref=dst.at[NEAR + (2 - rel) * NEAR + xc],
                send_sem=a_send.at[t], recv_sem=a_recv.at[t],
                device_id=(g, dev_at((zh + 1 + rel) % 4, n)), device_id_type=MESH).start()
            return 0

        lax.fori_loop(0, FAR, one, 0)

    def far_in(t):
        whole = into(t + 4, g)
        pltpu.make_async_copy(whole, whole, a_recv.at[t]).wait()

    def near_out(t):
        src = nsc if t == 3 else near.at[t]
        dst = gsc if t == 3 else gat.at[t]

        def one(k, _):
            n = (xc + k) % NEAR
            pltpu.make_async_remote_copy(
                src_ref=src.at[:, n], dst_ref=dst.at[:, xc],
                send_sem=x_send.at[t], recv_sem=x_recv.at[t],
                device_id=(g, dev_at(zh, n)), device_id_type=MESH).start()
            return 0

        lax.fori_loop(1, NEAR, one, 0)
        for n in range(NG):
            if t == 3:
                gsc[n, xc] = nsc[n, xc]
            else:
                gat[t, n, xc] = near[t, n, xc]

    def near_in(t):
        whole = (gsc if t == 3 else gat.at[t]).at[:, pl.ds(0, NEAR - 1)]
        pltpu.make_async_copy(whole, whole, x_recv.at[t]).wait()

    def maps():
        r = lax.broadcasted_iota(I32, (128, 128), 0)
        k = lax.broadcasted_iota(I32, (128, 128), 1)
        kin = k - (k // ROWS) * ROWS

        def piece(rem, size):
            return sum(((rem >= size * n).astype(I32) for n in range(1, NG)), jnp.zeros_like(rem))

        h1 = (r >= 48).astype(I32)
        rq = r - 48 * h1
        jq = piece(rq, 6)
        h2 = (r >= 112).astype(I32)
        rk = r - 96 - 16 * h2
        jk = piece(rk, 2)
        offset = jnp.where(r < 96, rq - 6 * jq + 6 * h1, rk - 2 * jk + 12 + 2 * h2)
        jmap[0] = jnp.where(offset == kin, jnp.where(r < 96, jq, jk), -1)
        jo = piece(r, 14)
        rv = r - 112
        jv = piece(rv, 2)
        offset = jnp.where(r < 112, r - 14 * jo, rv - 2 * jv + 14)
        jmap[1] = jnp.where(offset == kin, jnp.where(r < 112, jo, jv), -1)
        kg = lax.broadcasted_iota(I32, (ND, 128), 1) // ROWS
        held = jnp.zeros((ND, 128), I32)
        owner = own_ref[...].T
        for j in range(NG):
            held = held + jnp.where(owner[:, j:j + 1] == kg, j, 0)
        inv[...] = held

    def scales():
        at = lax.broadcasted_iota(I32, (ND, 128), 1) // ROWS
        lines = [gsc[n].reshape(ND, 128) for n in range(NG)]
        for t in range(3):
            held = jnp.zeros((ND, 128), F32)
            for n in range(NG):
                held = held + jnp.where(at == (n + t) % NG, lines[n], 0.0)
            sca[t] = pltpu.roll(held, (128 - ROWS * t) % 128, 1)

    def decode(t, pos):
        i = dev_at((zh + pos // NEAR) % 4, pos % NEAR)
        code = gat[t, :, pos].reshape(128, 128).astype(F32)
        hi = code.astype(BF16)
        lo = (code - hi.astype(F32)).astype(BF16)
        pick = jnp.where(jmap[min(t, 1)] == inv[pl.ds(i, 1), :], sca[t, pl.ds(pos, 1), :], 0.0).astype(BF16)
        got = jnp.dot(pick, jnp.concatenate([hi, lo], axis=1), preferred_element_type=F32)
        x = got[:, :128] + got[:, 128:]
        hi = x.astype(BF16)
        return i, hi, (x - hi.astype(F32)).astype(BF16)

    def decode_q(first, last):
        def one(pos, _):
            i, hi, lo = decode(0, pos)
            at = pl.ds(pl.multiple_of(i * 48, 16), 48)
            kat = pl.ds(pl.multiple_of(i * 16, 16), 16)
            for h in range(2):
                qm[h, at, 0:128] = hi[48 * h:48 * h + 48]
                qm[h, at, 128:256] = lo[48 * h:48 * h + 48]
                s = slice(96 + 16 * h, 112 + 16 * h)
                km[h, kat, 0:128] = hi[s]
                km[h, kat, 128:256] = hi[s]
                km[h, kat, 256:384] = lo[s]
            return 0

        lax.fori_loop(first, last, one, 0, unroll=4)

    def fold_q(h):
        def tile(i, _):
            at = pl.ds(pl.multiple_of(i * 768, 256), 768)
            x = nt(qm[h, at, :], km[h, :, 0:256]) + nt(qm[h, at, 0:128], km[h, :, 256:384])
            qf_ref[h, at, :] = x.astype(BF16)
            return 0

        lax.fori_loop(0, 2, tile, 0)

    def decode_o(h, first, last):
        om, vm = ((om0, vm0), (om1, vm1))[h]

        def one(pos, _):
            i, hi, lo = decode(1 + h, pos)
            at = pl.ds(pl.multiple_of(i * 112, 16), 112)
            vat = pl.ds(pl.multiple_of(i * 16, 16), 16)
            om[at, 0:128] = hi[:112]
            om[at, 128:256] = hi[:112]
            om[at, 256:384] = lo[:112]
            vm[vat, 0:128] = hi[112:]
            vm[vat, 128:256] = lo[112:]
            return 0

        lax.fori_loop(first, last, one, 0, unroll=4)

    def fold_o(first, last):
        def tile(i, _):
            at = pl.ds(pl.multiple_of(i * 256, 256), 256)
            of_ref[:, at] = fold_out(vm0, om0.at[at])
            return 0

        lax.fori_loop(first, last, tile, 0, unroll=2)

    order = (0, 3, 1, 2)
    for t in order:
        own(t)
    for t in order:
        far_out(t)
    maps()
    for t in order:
        partner(t)
    far_in(0)
    own(4)
    far_in(3)
    own(7)
    for t in order:
        forward(t, 0)
    partner(4)
    partner(7)
    for t in order:
        forward(t, 1)
    far_in(1)
    own(5)
    forward(4, 0)
    forward(7, 0)
    for t in order:
        finish(t)
        near_out(t)
    partner(5)
    forward(4, 1)
    forward(7, 1)
    far_in(2)
    own(6)
    partner(6)
    finish(7)
    near_in(3)
    scales()
    near_in(0)
    decode_q(0, NEAR)
    near_in(1)
    decode_o(0, 0, NEAR)
    near_in(2)
    decode_o(1, 0, NEAR)
    forward(5, 0)
    finish(4)
    decode_q(NEAR, ND)
    forward(5, 1)
    fold_q(0)
    forward(6, 0)
    fold_q(1)
    finish(5)
    decode_o(0, NEAR, ND)
    forward(6, 1)
    fold_o(0, 14)
    finish(6)
    decode_o(1, NEAR, ND)
    for c in started:
        c.wait_send()
    for t in range(4):
        sent = ssend if t == 3 else send.at[t]
        pltpu.make_async_copy(sent, sent, a_send.at[t]).wait()
        sent = (nsc if t == 3 else near.at[t]).at[:, pl.ds(0, NEAR - 1)]
        pltpu.make_async_copy(sent, sent, x_send.at[t]).wait()


def last_kernel(qf_ref, of_ref, om, vm, q_out, o_out, held, sem):
    whole = (pltpu.make_async_copy(qf_ref, q_out, sem.at[0]), pltpu.make_async_copy(of_ref, o_out.at[0], sem.at[1]))
    for c in whole:
        c.start()

    def out(i):
        at = pl.ds(pl.multiple_of(i * 256, 256), 256)
        return at, pltpu.make_async_copy(held.at[:, at], o_out.at[1, :, at], sem.at[2 + i])

    def tile(i, _):
        at, c = out(i)
        held[:, at] = fold_out(vm, om.at[at])
        c.start()
        return 0

    lax.fori_loop(0, 14, tile, 0, unroll=2)

    def done(i, _):
        out(i)[1].wait()
        return 0

    lax.fori_loop(0, 14, done, 0)
    for c in whole:
        c.wait()


def body(stored_q, stored_kv, stored_o, owner_map):
    vmem = pl.BlockSpec(memory_space=pltpu.VMEM)
    hbm = pl.BlockSpec(memory_space=pltpu.HBM)
    dma = pltpu.SemaphoreType.DMA
    far_inputs = [pltpu.with_memory_space_constraint(x, pltpu.HBM) for x in (
        stored_q.reshape(6, 64, 128),
        stored_kv.reshape(2, ND, 4, 128).transpose(1, 2, 0, 3).reshape(ND, 8, 128),
        stored_o.reshape(14, 64, 128))]
    parts = pl.pallas_call(
        kernel,
        out_shape=(pltpu.VMEM((2, 1536, 512), BF16), pltpu.VMEM((512, 3584), BF16),
                   pltpu.VMEM((3584, 384), BF16), pltpu.VMEM((512, 256), BF16)),
        in_specs=[hbm] * 3 + [vmem],
        out_specs=[vmem] * 4,
        scratch_shapes=[
            pltpu.VMEM((6, 64, 128), F32),
            pltpu.VMEM((ND, 8, 128), F32),
            pltpu.VMEM((14, 64, 128), F32),
            pltpu.VMEM((3, NG, NEAR, ROWS, 128), jnp.int16),
            pltpu.VMEM((NG, NEAR, 1, 128), F32),
            pltpu.VMEM((3, FAR, ROWS, 128), jnp.int16),
            pltpu.VMEM((FAR, 1, 128), F32),
            pltpu.VMEM((3, NG, ND, ROWS, 128), jnp.int16),
            pltpu.VMEM((NG, ND, 1, 128), F32),
            pltpu.VMEM((3, ND, 128), F32),
            pltpu.VMEM((2, 128, 128), I32),
            pltpu.VMEM((ND, 128), I32),
            pltpu.VMEM((2, 1536, 256), BF16),
            pltpu.VMEM((2, 512, 384), BF16),
            pltpu.VMEM((3584, 384), BF16),
            pltpu.VMEM((512, 256), BF16),
            dma((3,)), dma((4,)), dma((4,)), dma((4,)), dma((4,)), dma((72,)), dma((72,)),
        ],
        compiler_params=pltpu.CompilerParams(
            collective_id=0, has_side_effects=True, vmem_limit_bytes=32 * 1024 * 1024),
    )(*far_inputs, owner_map.T)
    return pl.pallas_call(
        last_kernel,
        out_shape=(jax.ShapeDtypeStruct((2, 1536, 512), BF16), jax.ShapeDtypeStruct((2, 512, 3584), BF16)),
        in_specs=[vmem] * 4,
        out_specs=[hbm] * 2,
        scratch_shapes=[pltpu.VMEM((512, 3584), BF16), dma((16,))],
        compiler_params=pltpu.CompilerParams(vmem_limit_bytes=32 * 1024 * 1024),
    )(*parts)


def solution(mesh):
    in_specs = (P("group", "dev", None), P("group", "dev", None), P("group", "dev", None), P())
    out_specs = (P("dev", None, None), P("dev", None, None))
    return jax.shard_map(body, mesh=mesh, in_specs=in_specs, out_specs=out_specs, check_vma=False)
```

time: 352 us -> 60.8 us (0.17)
  the two profiles are of different devices: /device:TPU:33 before, /device:TPU:6 now
where the time goes in v2:
time: 60.8 us; the launch traced here: 59.6 us
  Pallas kernels  58.3 us (96%)
  local copies, waits for them, and re-layouts  0.68 us (1%)
  between operations  0.65 us (1%)
    pallas_call x1, Pallas kernels, body(): pl.pallas_call(kernel, out_shape=(pltpu.VMEM((2, 1536, 512), BF16), pltpu...  54.2 us
    pallas_call x1, Pallas kernels, body(): pl.pallas_call(last_kernel, out_shape=(jax.ShapeDtypeStruct((2, 1536, 512...  4.11 us

profile of v2, /device:TPU:6, one launch (start us, length us, event | category | flops | bytes accessed | tf_op | source)
XLA Modules:
  0.0 59.6 jit_solution(5328422131580824745)
XLA Ops:
  0.6 0.0 copy-start
  0.6 0.7 %copy-done = s32[32,8]{0,1:T(8,128)S(1)} copy-done((s32[32,8]{0,1:T(8,128)S(1)}, s32[32,8]{0,1:T(8,128)}, u32[]{:S(2)}) %copy-start) | copy-done | bytes 1048
  1.3 54.2 %shard_map.59 = (bf16[2,1536,512]{2,1,0:T(8,128)(2,1)S(1)}, bf16[512,3584]{1,0:T(8,128)(2,1)S(1)}, bf16[3584,384]{1,0:T(8,128)(2,1)S(1)}, bf16[512,256]{1,0:T(8,128)(2,1)S(1)}) custom-call(f32[6,64,128]{2,1,0:T(8,128)} %bitcast.10, f32[32,8,128]{2,1,0:T(8,128)} %bitcast.11, f32[14,64,128]{2,1,0:T(8,128)} %bitcast.9, s32[8,32]{1,0:T(8,128)S(1)} %bitcast.8), custom_call_target="tpu_custom_call" | custom-call | tf_op jit(solution)/shard_map/pallas_call | solution.py:374
  55.5 4.1 %shard_map.60 = (bf16[2,1536,512]{2,1,0:T(8,128)(2,1)}, bf16[2,512,3584]{2,1,0:T(8,128)(2,1)}) custom-call(bf16[2,1536,512]{2,1,0:T(8,128)(2,1)S(1)} %get-tuple-element.6.qf_ref, bf16[512,3584]{1,0:T(8,128)(2,1)S(1)} %get-tuple-element.7.of_ref, bf16[3584,384]{1,0:T(8,128)(2,1)S(1)} %get-tuple-element.8.om, bf16[512,256]{1,0:T(8,128)(2,1)S(1)} %get-tuple-element.9.vm), custom_call_target="tpu_custom_call" | custom-call | tf_op jit(solution)/shard_map/pallas_call | solution.py:402
Async XLA Ops:
  0.6 0.7 %copy-start = (s32[32,8]{0,1:T(8,128)S(1)}, s32[32,8]{0,1:T(8,128)}, u32[]{:S(2)}) copy-start(s32[32,8]{0,1:T(8,128)} %param.7) | copy-start | bytes 3076

commit v3 on v2

--- a/solution.py
+++ b/solution.py
@@ -18,15 +18,16 @@
     return lax.dot_general(a, b, (((1,), (1,)), ((), ())), preferred_element_type=F32)
 
 
-def fold_out(v, o):
-    return (nt(v[:, 0:256], o[:, 0:256]) + nt(v[:, 0:128], o[:, 256:384])).astype(BF16)
-
-
-def kernel(q_hbm, kv_hbm, o_hbm, own_ref, qf_ref, of_ref, om1, vm1,
-           q_ref, kv_ref, o_ref, near, nsc, send, ssend, gat, gsc, sca, jmap, inv, qm, km, om0, vm0,
+def fold(a, b):
+    hi = b[:, 0:128]
+    return (nt(a, jnp.concatenate([hi, hi], axis=1)) + nt(a[:, 0:128], b[:, 128:256])).astype(BF16)
+
+
+def kernel(q_hbm, kv_hbm, o_hbm, own_hbm, qf_ref, of_ref, om1, vm1,
+           q_ref, kv_ref, o_ref, own_ref, near, nsc, send, ssend, gat, gsc, sca, jmap, inv, qm, km, om0, vm0,
            in_sem, a_send, a_recv, x_send, x_recv, s_send, s_recv):
     loads = [pltpu.make_async_copy(a, b, in_sem.at[n])
-             for n, (a, b) in enumerate(((q_hbm, q_ref), (kv_hbm, kv_ref), (o_hbm, o_ref)))]
+             for n, (a, b) in enumerate(((q_hbm, q_ref), (kv_hbm, kv_ref), (o_hbm, o_ref), (own_hbm, own_ref)))]
     for c in loads:
         c.start()
     g = lax.axis_index("group")
@@ -43,10 +44,14 @@
     barrier = pltpu.get_barrier_semaphore()
 
     def greet(i, _):
-        pl.semaphore_signal(barrier, inc=1, device_id=(g, (d + i) % ND), device_id_type=MESH)
+        who = dev_at((zh + 2 + i // NEAR) % 4, (xc + 4 + i) % NEAR)
+
+        @pl.when(who != d)
+        def _():
+            pl.semaphore_signal(barrier, inc=1, device_id=(g, who), device_id_type=MESH)
         return 0
 
-    lax.fori_loop(1, ND, greet, 0)
+    lax.fori_loop(0, ND, greet, 0)
     for who in (to_z, to_p, to_m):
         pl.semaphore_signal(barrier, inc=1, device_id=who, device_id_type=MESH)
 
@@ -87,8 +92,8 @@
 
     for c in loads:
         c.wait()
-    lax.fori_loop(0, NEAR, code_near, 0, unroll=2)
-    lax.fori_loop(0, FAR, code_far, 0, unroll=2)
+    lax.fori_loop(0, FAR, code_far, 0, unroll=4)
+    lax.fori_loop(0, NEAR, code_near, 0, unroll=4)
     pl.semaphore_wait(barrier, ND + 2)
 
     def into(part, group):
@@ -115,7 +120,13 @@
         started.append(c)
 
     def own(part):
+        own_z(part)
+        own_y(part)
+
+    def own_z(part):
         go(part, 0, into(part, g), to_z)
+
+    def own_y(part):
         go(part, 1, into(part, g), to_p)
         go(part, 2, into(part, g), to_m)
 
@@ -136,6 +147,19 @@
         for b, base in enumerate((mine, other)):
             hop(part, 5 + 2 * b, half(part, base + far, 0), to_p).wait_recv()
             hop(part, 6 + 2 * b, half(part, base + far, 1), to_m).wait_recv()
+
+    def cross(part):
+        go(part, 3, into(part, mine + down), to_z)
+        go(part, 4, into(part, mine + up), to_z)
+
+    def cross_far(part):
+        hop(part, 5, half(part, mine + far, 0), to_p).wait_recv()
+        hop(part, 6, half(part, mine + far, 1), to_m).wait_recv()
+        go(part, 7, into(part, mine + far), to_z)
+
+    def finish_cross(part):
+        for kind, group in ((0, y), (3, down), (4, up), (7, far)):
+            hop(part, kind, into(part, other + group), to_z).wait_recv()
 
     def far_out(t):
         src = ssend if t == 3 else send.at[t]
@@ -221,10 +245,13 @@
         hi = code.astype(BF16)
         lo = (code - hi.astype(F32)).astype(BF16)
         pick = jnp.where(jmap[min(t, 1)] == inv[pl.ds(i, 1), :], sca[t, pl.ds(pos, 1), :], 0.0).astype(BF16)
-        got = jnp.dot(pick, jnp.concatenate([hi, lo], axis=1), preferred_element_type=F32)
-        x = got[:, :128] + got[:, 128:]
+        x = jnp.dot(jnp.concatenate([pick, pick], axis=1), jnp.concatenate([hi, lo], axis=0),
+                    preferred_element_type=F32)
         hi = x.astype(BF16)
         return i, hi, (x - hi.astype(F32)).astype(BF16)
+
+    def over(first, last, one):
+        lax.fori_loop(first, last, one, 0, unroll=min(12, last - first))
 
     def decode_q(first, last):
         def one(pos, _):
@@ -234,22 +261,14 @@
             for h in range(2):
                 qm[h, at, 0:128] = hi[48 * h:48 * h + 48]
                 qm[h, at, 128:256] = lo[48 * h:48 * h + 48]
-                s = slice(96 + 16 * h, 112 + 16 * h)
-                km[h, kat, 0:128] = hi[s]
-                km[h, kat, 128:256] = hi[s]
-                km[h, kat, 256:384] = lo[s]
+                km[h, kat, 0:128] = hi[96 + 16 * h:112 + 16 * h]
+                km[h, kat, 128:256] = lo[96 + 16 * h:112 + 16 * h]
             return 0
 
-        lax.fori_loop(first, last, one, 0, unroll=4)
+        over(first, last, one)
 
     def fold_q(h):
-        def tile(i, _):
-            at = pl.ds(pl.multiple_of(i * 768, 256), 768)
-            x = nt(qm[h, at, :], km[h, :, 0:256]) + nt(qm[h, at, 0:128], km[h, :, 256:384])
-            qf_ref[h, at, :] = x.astype(BF16)
-            return 0
-
-        lax.fori_loop(0, 2, tile, 0)
+        qf_ref[h] = fold(qm[h], km[h])
 
     def decode_o(h, first, last):
         om, vm = ((om0, vm0), (om1, vm1))[h]
@@ -259,52 +278,55 @@
             at = pl.ds(pl.multiple_of(i * 112, 16), 112)
             vat = pl.ds(pl.multiple_of(i * 16, 16), 16)
             om[at, 0:128] = hi[:112]
-            om[at, 128:256] = hi[:112]
-            om[at, 256:384] = lo[:112]
+            om[at, 128:256] = lo[:112]
             vm[vat, 0:128] = hi[112:]
             vm[vat, 128:256] = lo[112:]
             return 0
 
-        lax.fori_loop(first, last, one, 0, unroll=4)
-
-    def fold_o(first, last):
+        over(first, last, one)
+
+    def fold_o():
         def tile(i, _):
             at = pl.ds(pl.multiple_of(i * 256, 256), 256)
-            of_ref[:, at] = fold_out(vm0, om0.at[at])
+            of_ref[:, at] = fold(vm0[...], om0[at])
             return 0
 
-        lax.fori_loop(first, last, tile, 0, unroll=2)
-
-    order = (0, 3, 1, 2)
+        lax.fori_loop(0, 14, tile, 0, unroll=14)
+
+    order = (3, 0, 1, 2)
     for t in order:
         own(t)
+    far_out(0)
+    far_out(3)
     for t in order:
-        far_out(t)
+        forward(t, 0)
+    for t in order:
+        partner(t)
+    far_out(1)
+    far_out(2)
     maps()
     for t in order:
-        partner(t)
+        forward(t, 1)
     far_in(0)
     own(4)
     far_in(3)
     own(7)
     for t in order:
-        forward(t, 0)
-    partner(4)
-    partner(7)
-    for t in order:
-        forward(t, 1)
+        finish(t)
+        near_out(t)
     far_in(1)
     own(5)
+    forward(7, 0)
     forward(4, 0)
-    forward(7, 0)
-    for t in order:
-        finish(t)
-        near_out(t)
-    partner(5)
-    forward(4, 1)
-    forward(7, 1)
+    partner(7)
+    partner(4)
     far_in(2)
     own(6)
+    forward(7, 1)
+    forward(4, 1)
+    forward(5, 0)
+    partner(5)
+    forward(6, 0)
     partner(6)
     finish(7)
     near_in(3)
@@ -315,17 +337,15 @@
     decode_o(0, 0, NEAR)
     near_in(2)
     decode_o(1, 0, NEAR)
-    forward(5, 0)
     finish(4)
     decode_q(NEAR, ND)
     forward(5, 1)
     fold_q(0)
-    forward(6, 0)
+    forward(6, 1)
     fold_q(1)
     finish(5)
     decode_o(0, NEAR, ND)
-    forward(6, 1)
-    fold_o(0, 14)
+    fold_o()
     finish(6)
     decode_o(1, NEAR, ND)
     for c in started:
@@ -348,11 +368,11 @@
 
     def tile(i, _):
         at, c = out(i)
-        held[:, at] = fold_out(vm, om.at[at])
+        held[:, at] = fold(vm[...], om[at])
         c.start()
         return 0
 
-    lax.fori_loop(0, 14, tile, 0, unroll=2)
+    lax.fori_loop(0, 14, tile, 0, unroll=14)
 
     def done(i, _):
         out(i)[1].wait()
@@ -370,17 +390,19 @@
     far_inputs = [pltpu.with_memory_space_constraint(x, pltpu.HBM) for x in (
         stored_q.reshape(6, 64, 128),
         stored_kv.reshape(2, ND, 4, 128).transpose(1, 2, 0, 3).reshape(ND, 8, 128),
-        stored_o.reshape(14, 64, 128))]
+        stored_o.reshape(14, 64, 128),
+        owner_map.T)]
     parts = pl.pallas_call(
         kernel,
         out_shape=(pltpu.VMEM((2, 1536, 512), BF16), pltpu.VMEM((512, 3584), BF16),
-                   pltpu.VMEM((3584, 384), BF16), pltpu.VMEM((512, 256), BF16)),
-        in_specs=[hbm] * 3 + [vmem],
+                   pltpu.VMEM((3584, 256), BF16), pltpu.VMEM((512, 256), BF16)),
+        in_specs=[hbm] * 4,
         out_specs=[vmem] * 4,
         scratch_shapes=[
             pltpu.VMEM((6, 64, 128), F32),
             pltpu.VMEM((ND, 8, 128), F32),
             pltpu.VMEM((14, 64, 128), F32),
+            pltpu.VMEM((NG, ND), I32),
             pltpu.VMEM((3, NG, NEAR, ROWS, 128), jnp.int16),
             pltpu.VMEM((NG, NEAR, 1, 128), F32),
             pltpu.VMEM((3, FAR, ROWS, 128), jnp.int16),
@@ -391,14 +413,14 @@
             pltpu.VMEM((2, 128, 128), I32),
             pltpu.VMEM((ND, 128), I32),
             pltpu.VMEM((2, 1536, 256), BF16),
-            pltpu.VMEM((2, 512, 384), BF16),
-            pltpu.VMEM((3584, 384), BF16),
+            pltpu.VMEM((2, 512, 256), BF16),
+            pltpu.VMEM((3584, 256), BF16),
             pltpu.VMEM((512, 256), BF16),
-            dma((3,)), dma((4,)), dma((4,)), dma((4,)), dma((4,)), dma((72,)), dma((72,)),
+            dma((4,)), dma((4,)), dma((4,)), dma((4,)), dma((4,)), dma((72,)), dma((72,)),
         ],
         compiler_params=pltpu.CompilerParams(
             collective_id=0, has_side_effects=True, vmem_limit_bytes=32 * 1024 * 1024),
-    )(*far_inputs, owner_map.T)
+    )(*far_inputs)
     return pl.pallas_call(
         last_kernel,
         out_shape=(jax.ShapeDtypeStruct((2, 1536, 512), BF16), jax.ShapeDtypeStruct((2, 512, 3584), BF16)),

time: 60.8 us -> 54.5 us (0.90)
  Pallas kernels: 58.3 us -> 53.2 us
  local copies, waits for them, and re-layouts: 0.68 us -> 0 us
    pallas_call x1, Pallas kernels: 54.2 us -> 49.1 us  [body(): pl.pallas_call(kernel, out_shape=(pltpu.VMEM((2, 1536, 512), BF16), pltpu...]
    unnamed x2 -> x0, local copies, waits for them, and re-layouts: 0.68 us -> none
where the time goes in v3:
time: 54.5 us; the launch traced here: 53.8 us
  Pallas kernels  53.2 us (98%)
  between operations  0.64 us (1%)
    pallas_call x1, Pallas kernels, body(): pl.pallas_call(kernel, out_shape=(pltpu.VMEM((2, 1536, 512), BF16), pltpu...  49.1 us
    pallas_call x1, Pallas kernels, body(): pl.pallas_call(last_kernel, out_shape=(jax.ShapeDtypeStruct((2, 1536, 512...  4.12 us

profile of v3, /device:TPU:6, one launch (start us, length us, event | category | flops | bytes accessed | tf_op | source)
XLA Modules:
  0.0 53.8 jit_solution(12879541764920507799)
XLA Ops:
  0.6 49.1 %shard_map.59 = (bf16[2,1536,512]{2,1,0:T(8,128)(2,1)S(1)}, bf16[512,3584]{1,0:T(8,128)(2,1)S(1)}, bf16[3584,256]{1,0:T(8,128)(2,1)S(1)}, bf16[512,256]{1,0:T(8,128)(2,1)S(1)}) custom-call(f32[6,64,128]{2,1,0:T(8,128)} %bitcast.9, f32[32,8,128]{2,1,0:T(8,128)} %bitcast.10, f32[14,64,128]{2,1,0:T(8,128)} %bitcast.8, s32[8,32]{1,0:T(8,128)} %bitcast.11), custom_call_target="tpu_custom_call" | custom-call | tf_op jit(solution)/shard_map/pallas_call | solution.py:395
  49.7 4.1 %shard_map.60 = (bf16[2,1536,512]{2,1,0:T(8,128)(2,1)}, bf16[2,512,3584]{2,1,0:T(8,128)(2,1)}) custom-call(bf16[2,1536,512]{2,1,0:T(8,128)(2,1)S(1)} %get-tuple-element.6.qf_ref, bf16[512,3584]{1,0:T(8,128)(2,1)S(1)} %get-tuple-element.7.of_ref, bf16[3584,256]{1,0:T(8,128)(2,1)S(1)} %get-tuple-element.8.om, bf16[512,256]{1,0:T(8,128)(2,1)S(1)} %get-tuple-element.9.vm), custom_call_target="tpu_custom_call" | custom-call | tf_op jit(solution)/shard_map/pallas_call | solution.py:424

commit v4 on v3

--- a/solution.py
+++ b/solution.py
@@ -322,12 +322,13 @@
     partner(4)
     far_in(2)
     own(6)
+    forward(5, 0)
+    cross(5)
     forward(7, 1)
     forward(4, 1)
-    forward(5, 0)
-    partner(5)
     forward(6, 0)
     partner(6)
+    cross_far(5)
     finish(7)
     near_in(3)
     scales()
@@ -339,11 +340,10 @@
     decode_o(1, 0, NEAR)
     finish(4)
     decode_q(NEAR, ND)
-    forward(5, 1)
     fold_q(0)
     forward(6, 1)
     fold_q(1)
-    finish(5)
+    finish_cross(5)
     decode_o(0, NEAR, ND)
     fold_o()
     finish(6)

time: 54.5 us -> 52.3 us (0.960)
  the two profiles are of different devices: /device:TPU:6 before, /device:TPU:1 now
where the time goes in v4:
time: 52.3 us; the launch traced here: 52.2 us
  Pallas kernels  51.6 us (99%)
  between operations  0.64 us (1%)
    pallas_call x1, Pallas kernels, body(): pl.pallas_call(kernel, out_shape=(pltpu.VMEM((2, 1536, 512), BF16), pltpu...  47.5 us
    pallas_call x1, Pallas kernels, body(): pl.pallas_call(last_kernel, out_shape=(jax.ShapeDtypeStruct((2, 1536, 512...  4.12 us

profile of v4, /device:TPU:1, one launch (start us, length us, event | category | flops | bytes accessed | tf_op | source)
XLA Modules:
  0.0 52.2 jit_solution(2816180347405142099)
XLA Ops:
  0.6 47.5 %shard_map.59 = (bf16[2,1536,512]{2,1,0:T(8,128)(2,1)S(1)}, bf16[512,3584]{1,0:T(8,128)(2,1)S(1)}, bf16[3584,256]{1,0:T(8,128)(2,1)S(1)}, bf16[512,256]{1,0:T(8,128)(2,1)S(1)}) custom-call(f32[6,64,128]{2,1,0:T(8,128)} %bitcast.9, f32[32,8,128]{2,1,0:T(8,128)} %bitcast.10, f32[14,64,128]{2,1,0:T(8,128)} %bitcast.8, s32[8,32]{1,0:T(8,128)} %bitcast.11), custom_call_target="tpu_custom_call" | custom-call | tf_op jit(solution)/shard_map/pallas_call | solution.py:395
  48.1 4.1 %shard_map.60 = (bf16[2,1536,512]{2,1,0:T(8,128)(2,1)}, bf16[2,512,3584]{2,1,0:T(8,128)(2,1)}) custom-call(bf16[2,1536,512]{2,1,0:T(8,128)(2,1)S(1)} %get-tuple-element.6.qf_ref, bf16[512,3584]{1,0:T(8,128)(2,1)S(1)} %get-tuple-element.7.of_ref, bf16[3584,256]{1,0:T(8,128)(2,1)S(1)} %get-tuple-element.8.om, bf16[512,256]{1,0:T(8,128)(2,1)S(1)} %get-tuple-element.9.vm), custom_call_target="tpu_custom_call" | custom-call | tf_op jit(solution)/shard_map/pallas_call | solution.py:424

commit v5 on v4

--- a/solution.py
+++ b/solution.py
@@ -9,6 +9,7 @@
 F32, BF16, I32 = jnp.float32, jnp.bfloat16, jnp.int32
 NG, ND = 8, 32
 ROWS = 16
+TILES, EARLY = 14, 7
 NEAR, FAR = 8, 24
 GROW = 1.008 / 32767.0
 LEAST = 2.0**-120
@@ -23,8 +24,8 @@
     return (nt(a, jnp.concatenate([hi, hi], axis=1)) + nt(a[:, 0:128], b[:, 128:256])).astype(BF16)
 
 
-def kernel(q_hbm, kv_hbm, o_hbm, own_hbm, qf_ref, of_ref, om1, vm1,
-           q_ref, kv_ref, o_ref, own_ref, near, nsc, send, ssend, gat, gsc, sca, jmap, inv, qm, km, om0, vm0,
+def kernel(q_hbm, kv_hbm, o_hbm, own_hbm, qf_ref, of_ref, om0, vm0, om1, vm1,
+           q_ref, kv_ref, o_ref, own_ref, near, nsc, send, ssend, gat, gsc, sca, jmap, inv, qm, km,
            in_sem, a_send, a_recv, x_send, x_recv, s_send, s_recv):
     loads = [pltpu.make_async_copy(a, b, in_sem.at[n])
              for n, (a, b) in enumerate(((q_hbm, q_ref), (kv_hbm, kv_ref), (o_hbm, o_ref), (own_hbm, own_ref)))]
@@ -291,7 +292,7 @@
             of_ref[:, at] = fold(vm0[...], om0[at])
             return 0
 
-        lax.fori_loop(0, 14, tile, 0, unroll=14)
+        lax.fori_loop(0, EARLY, tile, 0, unroll=EARLY)
 
     order = (3, 0, 1, 2)
     for t in order:
@@ -326,23 +327,23 @@
     cross(5)
     forward(7, 1)
     forward(4, 1)
-    forward(6, 0)
-    partner(6)
-    cross_far(5)
     finish(7)
     near_in(3)
     scales()
     near_in(0)
     decode_q(0, NEAR)
+    forward(6, 0)
+    partner(6)
     near_in(1)
     decode_o(0, 0, NEAR)
     near_in(2)
     decode_o(1, 0, NEAR)
+    cross_far(5)
     finish(4)
     decode_q(NEAR, ND)
     fold_q(0)
+    fold_q(1)
     forward(6, 1)
-    fold_q(1)
     finish_cross(5)
     decode_o(0, NEAR, ND)
     fold_o()
@@ -357,29 +358,20 @@
         pltpu.make_async_copy(sent, sent, x_send.at[t]).wait()
 
 
-def last_kernel(qf_ref, of_ref, om, vm, q_out, o_out, held, sem):
-    whole = (pltpu.make_async_copy(qf_ref, q_out, sem.at[0]), pltpu.make_async_copy(of_ref, o_out.at[0], sem.at[1]))
-    for c in whole:
+def last_kernel(qf_ref, of_ref, om0, vm0, om1, vm1, q_out, o_out, held, sem):
+    copies = [pltpu.make_async_copy(qf_ref, q_out, sem.at[0]),
+              pltpu.make_async_copy(of_ref, o_out.at[0, :, pl.ds(0, 256 * EARLY)], sem.at[1])]
+    for c in copies:
         c.start()
-
-    def out(i):
-        at = pl.ds(pl.multiple_of(i * 256, 256), 256)
-        return at, pltpu.make_async_copy(held.at[:, at], o_out.at[1, :, at], sem.at[2 + i])
-
-    def tile(i, _):
-        at, c = out(i)
-        held[:, at] = fold(vm[...], om[at])
+    for n in range(EARLY, 2 * TILES):
+        h, i = n // TILES, n % TILES
+        om, vm = ((om0, vm0), (om1, vm1))[h]
+        at = pl.ds(256 * i, 256)
+        held[h, :, at] = fold(vm[...], om[at])
+        c = pltpu.make_async_copy(held.at[h, :, at], o_out.at[h, :, at], sem.at[2 + n])
         c.start()
-        return 0
-
-    lax.fori_loop(0, 14, tile, 0, unroll=14)
-
-    def done(i, _):
-        out(i)[1].wait()
-        return 0
-
-    lax.fori_loop(0, 14, done, 0)
-    for c in whole:
+        copies.append(c)
+    for c in copies:
         c.wait()
 
 
@@ -394,10 +386,11 @@
         owner_map.T)]
     parts = pl.pallas_call(
         kernel,
-        out_shape=(pltpu.VMEM((2, 1536, 512), BF16), pltpu.VMEM((512, 3584), BF16),
+        out_shape=(pltpu.VMEM((2, 1536, 512), BF16), pltpu.VMEM((512, 256 * EARLY), BF16),
+                   pltpu.VMEM((3584, 256), BF16), pltpu.VMEM((512, 256), BF16),
                    pltpu.VMEM((3584, 256), BF16), pltpu.VMEM((512, 256), BF16)),
         in_specs=[hbm] * 4,
-        out_specs=[vmem] * 4,
+        out_specs=[vmem] * 6,
         scratch_shapes=[
             pltpu.VMEM((6, 64, 128), F32),
             pltpu.VMEM((ND, 8, 128), F32),
@@ -414,8 +407,6 @@
             pltpu.VMEM((ND, 128), I32),
             pltpu.VMEM((2, 1536, 256), BF16),
             pltpu.VMEM((2, 512, 256), BF16),
-            pltpu.VMEM((3584, 256), BF16),
-            pltpu.VMEM((512, 256), BF16),
             dma((4,)), dma((4,)), dma((4,)), dma((4,)), dma((4,)), dma((72,)), dma((72,)),
         ],
         compiler_params=pltpu.CompilerParams(
@@ -424,9 +415,9 @@
     return pl.pallas_call(
         last_kernel,
         out_shape=(jax.ShapeDtypeStruct((2, 1536, 512), BF16), jax.ShapeDtypeStruct((2, 512, 3584), BF16)),
-        in_specs=[vmem] * 4,
+        in_specs=[vmem] * 6,
         out_specs=[hbm] * 2,
-        scratch_shapes=[pltpu.VMEM((512, 3584), BF16), dma((16,))],
+        scratch_shapes=[pltpu.VMEM((2, 512, 3584), BF16), dma((2 + 2 * TILES,))],
         compiler_params=pltpu.CompilerParams(vmem_limit_bytes=32 * 1024 * 1024),
     )(*parts)
 

time: 52.3 us -> 51.6 us (0.987)
  the two profiles are of different devices: /device:TPU:1 before, /device:TPU:6 now
where the time goes in v5:
time: 51.6 us; the launch traced here: 51.5 us
  Pallas kernels  50.9 us (99%)
  between operations  0.64 us (1%)
    pallas_call x1, Pallas kernels, body(): pl.pallas_call(kernel, out_shape=(pltpu.VMEM((2, 1536, 512), BF16), pltpu...  46.6 us
    pallas_call x1, Pallas kernels, body(): pl.pallas_call(last_kernel, out_shape=(jax.ShapeDtypeStruct((2, 1536, 512...  4.26 us

profile of v5, /device:TPU:6, one launch (start us, length us, event | category | flops | bytes accessed | tf_op | source)
XLA Modules:
  0.0 51.5 jit_solution(14024233872065445858)
XLA Ops:
  0.6 46.6 %shard_map.59 = (bf16[2,1536,512]{2,1,0:T(8,128)(2,1)S(1)}, bf16[512,1792]{1,0:T(8,128)(2,1)S(1)}, bf16[3584,256]{1,0:T(8,128)(2,1)S(1)}, bf16[512,256]{1,0:T(8,...) custom-call(f32[6,64,128]{2,1,0:T(8,128)} %bitcast.9, f32[32,8,128]{2,1,0:T(8,128)} %bitcast.10, ...), custom_call_target="tpu_custom_call" | custom-call | tf_op jit(solution)/shard_map/pallas_call | solution.py:387
  47.2 4.3 %shard_map.60 = (bf16[2,1536,512]{2,1,0:T(8,128)(2,1)}, bf16[2,512,3584]{2,1,0:T(8,128)(2,1)}) custom-call(bf16[2,1536,512]{2,1,0:T(8,128)(2,1)S(1)} %get-tuple-element.8.qf_ref, bf16[512,1792]{1,0:T(8,128)(2,1)S(1)} %get-tuple-element.9.of_ref, bf16[3584,256]{1,0:T(8,128)(2,1)S(1)} %get-tuple-element.10.om0, bf16[512,256]{1,0:T(8,128)(2,1)S(1)} %get-tuple-element.11.vm0, ...), custom_call_target="tpu_custom_call" | custom-call | tf_op jit(solution)/shard_map/pallas_call | solution.py:415

commit v6 on v5

--- a/solution.py
+++ b/solution.py
@@ -327,13 +327,13 @@
     cross(5)
     forward(7, 1)
     forward(4, 1)
+    partner(6)
     finish(7)
     near_in(3)
     scales()
     near_in(0)
     decode_q(0, NEAR)
     forward(6, 0)
-    partner(6)
     near_in(1)
     decode_o(0, 0, NEAR)
     near_in(2)

time: 51.6 us -> 50.8 us (0.984)
  Pallas kernels: 50.9 us -> 50 us
    pallas_call x1, Pallas kernels: 46.6 us -> 45.8 us  [body(): pl.pallas_call(kernel, out_shape=(pltpu.VMEM((2, 1536, 512), BF16), pltpu...]
where the time goes in v6:
time: 50.8 us; the launch traced here: 50.7 us
  Pallas kernels  50 us (98%)
  between operations  0.64 us (1%)
    pallas_call x1, Pallas kernels, body(): pl.pallas_call(kernel, out_shape=(pltpu.VMEM((2, 1536, 512), BF16), pltpu...  45.8 us
    pallas_call x1, Pallas kernels, body(): pl.pallas_call(last_kernel, out_shape=(jax.ShapeDtypeStruct((2, 1536, 512...  4.26 us

profile of v6, /device:TPU:6, one launch (start us, length us, event | category | flops | bytes accessed | tf_op | source)
XLA Modules:
  0.0 50.7 jit_solution(886541346164723007)
XLA Ops:
  0.6 45.8 %shard_map.59 = (bf16[2,1536,512]{2,1,0:T(8,128)(2,1)S(1)}, bf16[512,1792]{1,0:T(8,128)(2,1)S(1)}, bf16[3584,256]{1,0:T(8,128)(2,1)S(1)}, bf16[512,256]{1,0:T(8,...) custom-call(f32[6,64,128]{2,1,0:T(8,128)} %bitcast.9, f32[32,8,128]{2,1,0:T(8,128)} %bitcast.10, ...), custom_call_target="tpu_custom_call" | custom-call | tf_op jit(solution)/shard_map/pallas_call | solution.py:387
  46.4 4.3 %shard_map.60 = (bf16[2,1536,512]{2,1,0:T(8,128)(2,1)}, bf16[2,512,3584]{2,1,0:T(8,128)(2,1)}) custom-call(bf16[2,1536,512]{2,1,0:T(8,128)(2,1)S(1)} %get-tuple-element.8.qf_ref, bf16[512,1792]{1,0:T(8,128)(2,1)S(1)} %get-tuple-element.9.of_ref, bf16[3584,256]{1,0:T(8,128)(2,1)S(1)} %get-tuple-element.10.om0, bf16[512,256]{1,0:T(8,128)(2,1)S(1)} %get-tuple-element.11.vm0, ...), custom_call_target="tpu_custom_call" | custom-call | tf_op jit(solution)/shard_map/pallas_call | solution.py:415

commit v7 on v6

--- a/solution.py
+++ b/solution.py
@@ -144,10 +144,13 @@
         hop(part, 2 + 2 * b, into(part, base + up), to_m).wait_recv()
         go(part, 6 + 2 * b, half(part, base + up, 1), to_m)
 
+    def finish_half(part, n):
+        for b, base in enumerate((mine, other)):
+            hop(part, 5 + 2 * b + n, half(part, base + far, n), (to_p, to_m)[n]).wait_recv()
+
     def finish(part):
-        for b, base in enumerate((mine, other)):
-            hop(part, 5 + 2 * b, half(part, base + far, 0), to_p).wait_recv()
-            hop(part, 6 + 2 * b, half(part, base + far, 1), to_m).wait_recv()
+        for n in range(2):
+            finish_half(part, n)
 
     def cross(part):
         go(part, 3, into(part, mine + down), to_z)
@@ -342,13 +345,14 @@
     finish(4)
     decode_q(NEAR, ND)
     fold_q(0)
+    forward(6, 1)
     fold_q(1)
-    forward(6, 1)
     finish_cross(5)
     decode_o(0, NEAR, ND)
     fold_o()
-    finish(6)
-    decode_o(1, NEAR, ND)
+    for n in range(2):
+        finish_half(6, n)
+        decode_o(1, NEAR + n * FAR // 2, NEAR + (n + 1) * FAR // 2)
     for c in started:
         c.wait_send()
     for t in range(4):

time: 50.8 us -> 50.7 us (level); the launches traced: 50.7 us -> 50 us
  Pallas kernels: 50 us -> 49.3 us
    pallas_call x1, Pallas kernels: 45.8 us -> 45.1 us  [body(): pl.pallas_call(kernel, out_shape=(pltpu.VMEM((2, 1536, 512), BF16), pltpu...]
where the time goes in v7:
time: 50.7 us; the launch traced here: 50 us
  Pallas kernels  49.3 us (97%)
  between operations  0.64 us (1%)
    pallas_call x1, Pallas kernels, body(): pl.pallas_call(kernel, out_shape=(pltpu.VMEM((2, 1536, 512), BF16), pltpu...  45.1 us
    pallas_call x1, Pallas kernels, body(): pl.pallas_call(last_kernel, out_shape=(jax.ShapeDtypeStruct((2, 1536, 512...  4.26 us

profile of v7, /device:TPU:6, one launch (start us, length us, event | category | flops | bytes accessed | tf_op | source)
XLA Modules:
  0.0 50.0 jit_solution(17133652468603274882)
XLA Ops:
  0.6 45.1 %shard_map.59 = (bf16[2,1536,512]{2,1,0:T(8,128)(2,1)S(1)}, bf16[512,1792]{1,0:T(8,128)(2,1)S(1)}, bf16[3584,256]{1,0:T(8,128)(2,1)S(1)}, bf16[512,256]{1,0:T(8,...) custom-call(f32[6,64,128]{2,1,0:T(8,128)} %bitcast.9, f32[32,8,128]{2,1,0:T(8,128)} %bitcast.10, ...), custom_call_target="tpu_custom_call" | custom-call | tf_op jit(solution)/shard_map/pallas_call | solution.py:391
  45.7 4.3 %shard_map.60 = (bf16[2,1536,512]{2,1,0:T(8,128)(2,1)}, bf16[2,512,3584]{2,1,0:T(8,128)(2,1)}) custom-call(bf16[2,1536,512]{2,1,0:T(8,128)(2,1)S(1)} %get-tuple-element.8.qf_ref, bf16[512,1792]{1,0:T(8,128)(2,1)S(1)} %get-tuple-element.9.of_ref, bf16[3584,256]{1,0:T(8,128)(2,1)S(1)} %get-tuple-element.10.om0, bf16[512,256]{1,0:T(8,128)(2,1)S(1)} %get-tuple-element.11.vm0, ...), custom_call_target="tpu_custom_call" | custom-call | tf_op jit(solution)/shard_map/pallas_call | solution.py:419
